TPU v7x, 512 devices: a whole 4x4x16 slice. The times are simulated.
512 devices in a mesh: px: 64 (over y, z_hi, x, core), pz: 8 (over z_lo).
Axes of the slice: x: 4, y: 4, z: 16 (z_hi: 2, z_lo: 8; z = z_hi * 8 + z_lo), core: 2. Of those that a mesh axis runs over, the one named last changes fastest.
Arguments:
- wall_vel: bfloat16 [512, 512, 192], P('pz', 'px'), may hold values from -1.1953125 to 1.1953125
- wall_slope: bfloat16 [512, 512, 192], P('pz', 'px'), may hold values from -600 to 600
- wall_curvature: bfloat16 [512, 512, 192], P('pz', 'px'), may hold values from -600 to 600
- vorticity: bfloat16 [512, 512, 192], P('pz', 'px'), may hold values from -6 to 6
- vort_slope: bfloat16 [512, 512, 192], P('pz', 'px'), may hold values from -60 to 60
- mean_profile: float32 [4, 192], replicated, may hold values from -1200 to 1200
- eigen_basis: bfloat16 [192, 192], replicated, as said below
- eigen_decay: float32 [192], replicated, may hold values from 0 to 4, as said below
- viscous_step: float32 [1], replicated, may hold values from 0.0001 to 0.0004
- time_step: float32 [1], replicated, may hold values from 0.01 to 0.03
Outputs:
- vorticity_next: bfloat16 [512, 512, 192], P('pz', 'px')
Inputs may be any that keep to these rules, and one draw needn't show every extreme that they name: `eigen_basis`: the columns are orthonormal eigenvectors of the second difference over 192 points with zero wall values, in some order and with some signs, rounded. `eigen_decay`: one positive factor times the eigenvalue magnitude of the matching column of eigen_basis.
All inputs are finite; a program needn't handle non-finite values.
Results may differ from a plain program's by a relative error of at most 0.011.
Values may be sent and summed in bfloat16 or wider, within the bound.
A program may use at most 128 MiB of HBM per device.

v0:
```python
import functools
import math

import jax
import jax.numpy as jnp
import ml_dtypes
import numpy as np
from jax import lax
from jax.experimental import pallas as pl
from jax.experimental.pallas import tpu as pltpu
from jax.sharding import PartitionSpec as P

NR = 8
WALLS = 3
FIELDS = 5
QUADS = 4
KZB = 64
KXB = 8

STREAM_SCALE = 0.25
SPAN_SCALE = 2.0 / 3.0
EXPLICIT = 29.0 / 96.0
IMPLICIT = 37.0 / 160.0
FORCING = 8.0 / 15.0

BF = jnp.bfloat16
F32 = jnp.float32

SLOPE, CURV, VORT, VSLOPE, VEL = range(FIELDS)


def make_tables(count, points, scale):
    indices = np.arange(count)
    number = indices // 2
    cosine = (indices % 2 == 0)[:, None]
    phase = number[:, None] * np.arange(points)[None, :] % points
    angles = phase * (2.0 * math.pi / points)
    cos_part, sin_part = np.cos(angles), np.sin(angles)
    shape_rows = np.where(cosine, cos_part, sin_part)
    norm = math.sqrt(2.0 / count)
    synthesis = norm * shape_rows
    analysis = (2.0 / points / norm * shape_rows).T
    slope_rows = np.where(cosine, sin_part, -cos_part)
    slope_analysis = ((scale * number)[:, None] * (2.0 / points / norm) * slope_rows).T

    def rounded(t):
        return t.astype(np.float32).astype(ml_dtypes.bfloat16)

    return rounded(synthesis), rounded(analysis), rounded(slope_analysis)


def all_tables(ng, nr, npz):
    kxb = KXB * ng
    nkx, nkz = kxb * nr, KZB * npz
    syn_x, ana_x, slope_x = make_tables(nkx, nkx * 3 // 2, STREAM_SCALE)
    syn_z, ana_z, slope_z = make_tables(nkz, nkz * 3 // 2, SPAN_SCALE)
    r, c, m, g = np.meshgrid(
        np.arange(nr), np.arange(QUADS), np.arange(2), np.arange(ng), indexing="ij"
    )
    order = (g * (KXB * nr) + r * KXB + 2 * c + m).reshape(nr, kxb)
    plain = order.reshape(-1)
    crossed = order.reshape(nr // 2, 2, kxb)[:, ::-1].reshape(-1)
    rows = KZB * KXB
    move = np.zeros((rows, rows), np.float32)
    kz, kx = np.meshgrid(np.arange(KZB), np.arange(KXB), indexing="ij")
    move[(kz * KXB + kx).reshape(-1), (kx * KZB + kz).reshape(-1)] = 1.0
    return (
        move.astype(ml_dtypes.bfloat16),
        np.ascontiguousarray(syn_z.T),
        np.ascontiguousarray(syn_x[plain]),
        np.ascontiguousarray(syn_x[crossed]),
        np.ascontiguousarray(slope_x[:, plain]),
        np.ascontiguousarray(ana_x[:, crossed]),
        ana_z,
        slope_z,
    )


def dot(a, b, ca, cb):
    return lax.dot_general(a, b, (((ca,), (cb,)), ((), ())), preferred_element_type=F32)


def kernel_body(
    ng, nr, npz,
    slope_h, curv_h, vort_h, vslope_h, vel_h,
    move_h, synz_h, synx0_h, synx1_h, slopex_h, anax_h, anaz_h, slopez_h,
    mean_ref, basis_ref, decay_ref, visc_ref, dt_ref,
    out_ref,
    xin, move, synz, synx0, synx1, slopex, anax, anaz, slopez,
    stage, send_a, recv_a, wide, coef, mixed_rows, send_b, recv_b, lhs, flux,
    send_c, recv_c, back, send_d, recv_d, old, spread,
    in_sem, tab_sem, own_sem, sa_sem, ra_sem, sb_sem, rb_sem, sc_sem, rc_sem, sd_sem, rd_sem,
):
    owners = ng * npz
    kxl = KXB * ng
    zb = synz.shape[0] // nr
    px = lax.axis_index("px")
    pz = lax.axis_index("pz")
    g = px // nr
    r = px % nr
    me = pz * ng + g
    par = r % 2

    def owner(s):
        return {"px": (s % ng) * nr + r, "pz": s // ng}

    def peer(q):
        return {"px": g * nr + q, "pz": pz}

    ins = [
        pltpu.make_async_copy(h, xin.at[i], in_sem.at[i])
        for i, h in enumerate((slope_h, curv_h, vort_h, vslope_h, vel_h))
    ]
    tabs = [
        pltpu.make_async_copy(h, v, tab_sem.at[i])
        for i, (h, v) in enumerate(
            (
                (move_h, move), (synz_h, synz), (synx0_h, synx0), (synx1_h, synx1),
                (slopex_h, slopex), (anax_h, anax), (anaz_h, anaz), (slopez_h, slopez),
            )
        )
    ]
    tabs[0].start()
    for copy in ins:
        copy.start()
    for copy in tabs[1:]:
        copy.start()

    barrier = pltpu.get_barrier_semaphore()

    @pl.loop(1, owners)
    def _(t):
        pl.semaphore_signal(
            barrier, inc=1, device_id=owner((me + t) % owners),
            device_id_type=pl.DeviceIdType.MESH,
        )

    @pl.loop(1, nr)
    def _(t):
        pl.semaphore_signal(
            barrier, inc=1, device_id=peer((r + t) % nr),
            device_id_type=pl.DeviceIdType.MESH,
        )

    tabs[0].wait()
    per_owner = FIELDS * QUADS
    for i in range(FIELDS):
        ins[i].wait()
        block = xin[i].reshape(KZB * KXB, xin.shape[3])
        turned = dot(block, move[...], 0, 0)
        for j in range(WALLS):
            for c in range(QUADS):
                stage[pl.ds(j * owners * per_owner + i * QUADS + c, owners, stride=per_owner), :] = (
                    turned[j * owners : (j + 1) * owners, 128 * c : 128 * c + 128]
                )
        if i == VORT:
            old[...] = dot(basis_ref[...], turned.astype(BF), 0, 0)

    for j in range(WALLS):
        rows = owners * per_owner
        send_a[j] = (
            stage[j * rows : (j + 1) * rows, :].astype(BF).reshape(owners, FIELDS, QUADS, 128)
        )

    pl.semaphore_wait(barrier, owners - 1 + nr - 1)

    for j in range(WALLS):
        pltpu.make_async_copy(send_a.at[j, me], recv_a.at[j, me], ra_sem.at[j]).start()

        @pl.loop(1, owners)
        def _(t, j=j):
            to = (me + t) % owners
            pltpu.make_async_remote_copy(
                src_ref=send_a.at[j, to], dst_ref=recv_a.at[j, me],
                send_sem=sa_sem.at[j], recv_sem=ra_sem.at[j],
                device_id=owner(to), device_id_type=pl.DeviceIdType.MESH,
            ).start()

    row = lax.broadcasted_iota(jnp.int32, (owners, 128), 0)
    lane = lax.broadcasted_iota(jnp.int32, (owners, 128), 1)
    lower = lane < KZB
    even = lane % 2 == 0
    kz_rate = SPAN_SCALE * ((KZB // 2) * (row // ng) + (lane % KZB) // 2).astype(F32)
    fz = jnp.where(even, kz_rate, -kz_rate)
    for c in range(QUADS):
        number = (KXB // 2) * nr * (row % ng) + (KXB // 2) * r + c
        kx_rate = STREAM_SCALE * number.astype(F32)
        fx = jnp.where(lower, kx_rate, -kx_rate)
        square = kx_rate * kx_rate + kz_rate * kz_rate
        safe = jnp.where(square == 0.0, 1.0, square)
        coef[c, 0] = fx
        coef[c, 1] = fx / safe
        coef[c, 2] = fz / safe
    coef[0, 3] = fz

    points = basis_ref.shape[0]
    col = lax.broadcasted_iota(jnp.int32, (points, points * QUADS), 1)
    point = lax.broadcasted_iota(jnp.int32, (points, points * QUADS), 0)
    wide_basis = dot(
        basis_ref[...], jnp.where(col // QUADS == point, 1.0, 0.0).astype(BF), 0, 0
    )
    for c in range(QUADS):
        spread[c * points : (c + 1) * points, :] = jnp.where(
            col % QUADS == c, wide_basis, 0.0
        ).astype(BF)

    def swap_x(v):
        return pltpu.roll(v, KZB, 1)

    def swap_z(v):
        return jnp.where(even, pltpu.roll(v, 127, 1), pltpu.roll(v, 1, 1))

    first = (row == 0) & (lane == 0) & (px == g * nr) & (r == 0)

    def forward(j):
        pltpu.make_async_copy(recv_a.at[j], recv_a.at[j], ra_sem.at[j]).wait()
        wide[...] = recv_a[j].reshape(owners * per_owner, 128).astype(F32)
        if j == 0:
            tabs[1].wait()
        for c in range(QUADS):
            def load(i, c=c):
                return wide[pl.ds(i * QUADS + c, owners, stride=per_owner), :]

            s, cv, o, q, v = (load(i) for i in range(FIELDS))
            fx, a, b, fzz = coef[c, 0], coef[c, 1], coef[c, 2], coef[0, 3]
            stream_vel = swap_z(b * o) - swap_x(a * s)
            span_vel = -swap_z(b * s) - swap_x(a * o)
            stream_vort = swap_z(fzz * v - b * cv) - swap_x(a * q)
            span_vort = swap_x(a * cv - fx * v) - swap_z(b * q)
            if c == 0:
                def mean(i):
                    return jnp.where(first, mean_ref[i, owners * j + me], 0.0)

                stream_vel += mean(0)
                span_vel += mean(1)
                stream_vort += mean(3)
                span_vort -= mean(2)
            for f, field in enumerate((stream_vel, span_vel, v, stream_vort, o, span_vort)):
                at = pl.multiple_of((f + par - 2 * par * (f % 2)) * kxl + c * 2 * ng, 2 * ng)
                low, high = [], []
                for p in range(npz // 2):
                    one = field[2 * p * ng : (2 * p + 1) * ng]
                    two = field[(2 * p + 1) * ng : (2 * p + 2) * ng]
                    keep = lower[:ng]
                    low.append(jnp.where(keep, one, pltpu.roll(two, KZB, 1)))
                    high.append(jnp.where(keep, pltpu.roll(one, KZB, 1), two))
                packed = jnp.concatenate(
                    [jnp.concatenate(low, axis=1), jnp.concatenate(high, axis=1)], axis=0
                )
                mixed_rows[pl.ds(at, 2 * ng), :] = packed.astype(BF)
        send_b[j] = dot(synz[...], mixed_rows[...], 1, 1).astype(BF)
        pltpu.make_async_copy(
            send_b.at[j, pl.ds(pl.multiple_of(r * zb, zb), zb)], recv_b.at[j, r], rb_sem.at[j]
        ).start()

        @pl.loop(1, nr)
        def _(t):
            to = (r + t) % nr
            pltpu.make_async_remote_copy(
                src_ref=send_b.at[j, pl.ds(pl.multiple_of(to * zb, zb), zb)],
                dst_ref=recv_b.at[j, r],
                send_sem=sb_sem.at[j], recv_sem=rb_sem.at[j],
                device_id=peer(to), device_id_type=pl.DeviceIdType.MESH,
            ).start()

    half = lax.broadcasted_iota(jnp.int32, (zb, 2 * kxl), 1) < kxl
    nxp = synx0.shape[1]
    step = min(256, nxp)

    def middle(j):
        pltpu.make_async_copy(recv_b.at[j], recv_b.at[j], rb_sem.at[j]).wait()
        for b in range(3):
            at = slice(2 * b * kxl, 2 * (b + 1) * kxl)
            for p in range(nr // 2):
                one, two = recv_b[j, 2 * p, :, at], recv_b[j, 2 * p + 1, :, at]
                to = slice(2 * p * kxl, 2 * (p + 1) * kxl)
                lhs[2 * b, :, to] = jnp.where(half, one, two)
                lhs[2 * b + 1, :, to] = jnp.where(half, two, one)
        if j == 0:
            for copy in tabs[2:6]:
                copy.wait()
        for n in range(0, nxp, step):
            cut = slice(n, n + step)
            grid = [
                dot(lhs[f], (synx0 if f % 2 == 0 else synx1)[:, cut], 1, 0) for f in range(6)
            ]
            flux[0, :, cut] = (grid[0] * grid[4] - grid[2] * grid[3]).astype(BF)
            flux[1, :, cut] = (grid[1] * grid[4] - grid[2] * grid[5]).astype(BF)
        for p in range(nr // 2):
            cut = slice(2 * p * kxl, 2 * (p + 1) * kxl)
            stream_part = dot(flux[0], slopex[:, cut], 1, 0)
            span_part = dot(flux[1], anax[:, cut], 1, 0)
            send_c[j, 2 * p] = jnp.where(half, stream_part, span_part).astype(BF)
            send_c[j, 2 * p + 1] = jnp.where(half, span_part, stream_part).astype(BF)
        pltpu.make_async_copy(send_c.at[j, r], recv_c.at[j, r], rc_sem.at[j]).start()

        @pl.loop(1, nr)
        def _(t):
            to = (r + t) % nr
            pltpu.make_async_remote_copy(
                src_ref=send_c.at[j, to], dst_ref=recv_c.at[j, r],
                send_sem=sc_sem.at[j], recv_sem=rc_sem.at[j],
                device_id=peer(to), device_id_type=pl.DeviceIdType.MESH,
            ).start()

    def backward(j):
        pltpu.make_async_copy(recv_c.at[j], recv_c.at[j], rc_sem.at[j]).wait()
        if j == 0:
            for copy in tabs[6:8]:
                copy.wait()
        parts = recv_c[j].reshape(nr * zb, 2 * kxl)
        one = dot(parts, anaz[...], 0, 0)
        two = dot(parts, slopez[...], 0, 0)
        nonlinear = -jnp.where(par == 0, one[:kxl] + two[kxl:], one[kxl:] + two[:kxl])
        keep = lower[:ng]
        for c in range(QUADS):
            for p in range(npz // 2):
                cut = slice(128 * p, 128 * p + 128)
                low = nonlinear[2 * c * ng : (2 * c + 1) * ng, cut]
                high = nonlinear[(2 * c + 1) * ng : (2 * c + 2) * ng, cut]
                back[pl.ds(2 * p * ng * QUADS + c, ng, stride=QUADS), :] = jnp.where(
                    keep, low, pltpu.roll(high, KZB, 1)
                )
                back[pl.ds((2 * p + 1) * ng * QUADS + c, ng, stride=QUADS), :] = jnp.where(
                    keep, pltpu.roll(low, KZB, 1), high
                )
        send_d[j] = back[...].astype(BF).reshape(owners, QUADS, 128)
        pltpu.make_async_copy(send_d.at[j, me], recv_d.at[j, me], rd_sem.at[j]).start()

        @pl.loop(1, owners)
        def _(t):
            to = (me + t) % owners
            pltpu.make_async_remote_copy(
                src_ref=send_d.at[j, to], dst_ref=recv_d.at[j, me],
                send_sem=sd_sem.at[j], recv_sem=rd_sem.at[j],
                device_id=owner(to), device_id_type=pl.DeviceIdType.MESH,
            ).start()

    forward(0)
    middle(0)
    forward(1)
    backward(0)
    middle(1)
    forward(2)
    backward(1)
    middle(2)
    backward(2)

    lane1 = lax.broadcasted_iota(jnp.int32, (1, 128), 1)
    kz1 = SPAN_SCALE * ((KZB // 2) * pz + (lane1 % KZB) // 2).astype(F32)
    kz_square = kz1 * kz1
    for j in range(WALLS):
        pltpu.make_async_copy(recv_d.at[j], recv_d.at[j], rd_sem.at[j]).wait()
    returned = recv_d[...].reshape(points * QUADS, 128)
    flux_coef = dot(spread[...], returned, 1, 0)
    decay = decay_ref[...]
    pieces = []
    for c in range(QUADS):
        kx1 = STREAM_SCALE * ((KXB // 2) * px + c).astype(F32)
        rates = decay + visc_ref[0] * (kz_square + kx1 * kx1)
        denom = 1.0 + IMPLICIT * rates
        old_coef = old[:, 128 * c : 128 * c + 128]
        new_coef = flux_coef[c * points : (c + 1) * points]
        mixed = (1.0 - EXPLICIT * rates) / denom * old_coef + FORCING * dt_ref[0] / denom * new_coef
        pieces.append(dot(basis_ref[...], mixed.astype(BF), 1, 0).astype(BF))
    result = dot(move[...], jnp.concatenate(pieces, axis=1), 1, 1)
    out_ref[...] = result.reshape(KZB, KXB, points).astype(BF)

    for j in range(WALLS):
        pltpu.make_async_copy(
            send_a.at[j, pl.ds(0, owners - 1)], send_a.at[j, pl.ds(0, owners - 1)], sa_sem.at[j]
        ).wait()
        pltpu.make_async_copy(
            recv_b.at[j, pl.ds(0, nr - 1)], recv_b.at[j, pl.ds(0, nr - 1)], sb_sem.at[j]
        ).wait()
        pltpu.make_async_copy(
            send_c.at[j, pl.ds(0, nr - 1)], send_c.at[j, pl.ds(0, nr - 1)], sc_sem.at[j]
        ).wait()
        pltpu.make_async_copy(
            send_d.at[j, pl.ds(0, owners - 1)], send_d.at[j, pl.ds(0, owners - 1)], sd_sem.at[j]
        ).wait()


def per_device(
    ng, nr, npz, tables,
    wall_vel, wall_slope, wall_curvature, vorticity, vort_slope,
    mean_profile, eigen_basis, eigen_decay, viscous_step, time_step,
):
    owners = ng * npz
    kxl = KXB * ng
    nkx, nkz = kxl * nr, KZB * npz
    nxp, nzp = nkx * 3 // 2, nkz * 3 // 2
    zb = nzp // nr
    points = WALLS * owners
    lanes = KZB * KXB
    hbm = pl.BlockSpec(memory_space=pl.ANY)
    vmem = pl.BlockSpec(memory_space=pltpu.VMEM)
    smem = pl.BlockSpec(memory_space=pltpu.SMEM)
    dma = pltpu.SemaphoreType.DMA
    scratch = [
        pltpu.VMEM((FIELDS, KZB, KXB, points), BF),
        *[pltpu.VMEM(t.shape, BF) for t in tables],
        pltpu.VMEM((WALLS * owners * FIELDS * QUADS, 128), F32),
        pltpu.VMEM((WALLS, owners, FIELDS, QUADS, 128), BF),
        pltpu.VMEM((WALLS, owners, FIELDS, QUADS, 128), BF),
        pltpu.VMEM((owners * FIELDS * QUADS, 128), F32),
        pltpu.VMEM((QUADS, 4, owners, 128), F32),
        pltpu.VMEM((6 * kxl, nkz), BF),
        pltpu.VMEM((WALLS, nzp, 6 * kxl), BF),
        pltpu.VMEM((WALLS, nr, zb, 6 * kxl), BF),
        pltpu.VMEM((6, zb, nkx), BF),
        pltpu.VMEM((2, zb, nxp), BF),
        pltpu.VMEM((WALLS, nr, zb, 2 * kxl), BF),
        pltpu.VMEM((WALLS, nr, zb, 2 * kxl), BF),
        pltpu.VMEM((owners * QUADS, 128), F32),
        pltpu.VMEM((WALLS, owners, QUADS, 128), BF),
        pltpu.VMEM((WALLS, owners, QUADS, 128), BF),
        pltpu.VMEM((points, lanes), F32),
        pltpu.VMEM((points * QUADS, points * QUADS), BF),
        dma((FIELDS,)),
        dma((len(tables),)),
        dma((1,)),
        *[dma((WALLS,)) for _ in range(8)],
    ]
    return pl.pallas_call(
        functools.partial(kernel_body, ng, nr, npz),
        out_shape=jax.ShapeDtypeStruct(vorticity.shape, BF),
        in_specs=[hbm] * (FIELDS + len(tables)) + [smem, vmem, vmem, smem, smem],
        out_specs=vmem,
        scratch_shapes=scratch,
        compiler_params=pltpu.CompilerParams(
            collective_id=0, has_side_effects=True, vmem_limit_bytes=56 * 1024 * 1024
        ),
    )(
        wall_slope, wall_curvature, vorticity, vort_slope, wall_vel,
        *[jnp.asarray(t) for t in tables],
        mean_profile, eigen_basis, eigen_decay[:, None], viscous_step, time_step,
    )


def build(mesh, nr):
    npz = mesh.shape["pz"]
    ng = mesh.shape["px"] // nr
    tables = all_tables(ng, nr, npz)
    spec = P("pz", "px", None)
    return jax.shard_map(
        functools.partial(per_device, ng, nr, npz, tables),
        mesh=mesh,
        in_specs=(spec,) * 5 + (P(),) * 5,
        out_specs=spec,
        check_vma=False,
    )


def solution(mesh):
    return build(mesh, NR)
```

profile of v0, /device:TPU:1, one launch (start us, length us, event | category | flops | bytes accessed | tf_op | source)
XLA Modules:
  0.0 101.3 jit_solution(5023241942829414255)
XLA Ops:
  1.3 0.0 copy-start
  1.3 0.7 copy-done
  2.0 0.8 copy.19.decay_ref
  2.7 96.9 %shard_map.172 = bf16[64,8,192]{2,1,0:T(8,128)(2,1)} custom-call(bf16[64,8,192]{2,1,0:T(8,128)(2,1)} %slope_h.1, bf16[64,8,192]{2,1,0:T(8,128)(2,1)} %curv_h.1, bf16[64,8,192]{2,1,0:T(8,128)(2,1)} %vort_h.1, bf16[64,8,192]{2,1,0:T(8,128)(2,1)} %vslope_h.1, bf16[64,8,192]{2,1,0:T(8,128)(2,1)} %vel_h.1, bf16[512,512]{1,0:T(8,128)(2,1)} %constant.16.clone.move_h, ...), custom_call_target="tpu_custom_call" | custom-call | tf_op jit(solution)/shard_map/pallas_call | solution.py:425
  99.6 1.7 %copy.23 = bf16[64,8,192]{2,1,0:T(8,128)(2,1)} copy(bf16[64,8,192]{2,1,0:T(8,128)(2,1)} %shard_map.172) | data formatting | bytes 393216
Async XLA Ops:
  1.3 0.7 copy-start
where the time goes:
time: 102 us; the launch traced here: 101 us
  Pallas kernels  96.9 us (95%)
  local copies, waits for them, and re-layouts  3.11 us (3%)
  between operations  1.31 us (1%)
    pallas_call x1, Pallas kernels, per_device(): pl.pallas_call(functools.partial(kernel_body, ng, nr, npz), out_shape=jax...  96.9 us
    unnamed x3, local copies, waits for them, and re-layouts  2.34 us

commit v1 on v0

v1 whole, which is shorter than its diff:
```python
import functools
import math

import jax
import jax.numpy as jnp
import ml_dtypes
import numpy as np
from jax import lax
from jax.experimental import pallas as pl
from jax.experimental.pallas import tpu as pltpu
from jax.sharding import PartitionSpec as P

NR = 8
WALLS = 3
FIELDS = 5
QUADS = 4
KZB = 64
KXB = 8

STREAM_SCALE = 0.25
SPAN_SCALE = 2.0 / 3.0
EXPLICIT = 29.0 / 96.0
IMPLICIT = 37.0 / 160.0
FORCING = 8.0 / 15.0

BF = jnp.bfloat16
F32 = jnp.float32

SLOPE, VORT, VEL, CURV, VSLOPE = range(FIELDS)
EARLY = 3


def make_tables(count, points, scale):
    indices = np.arange(count)
    number = indices // 2
    cosine = (indices % 2 == 0)[:, None]
    phase = number[:, None] * np.arange(points)[None, :] % points
    angles = phase * (2.0 * math.pi / points)
    cos_part, sin_part = np.cos(angles), np.sin(angles)
    shape_rows = np.where(cosine, cos_part, sin_part)
    norm = math.sqrt(2.0 / count)
    synthesis = norm * shape_rows
    analysis = (2.0 / points / norm * shape_rows).T
    slope_rows = np.where(cosine, sin_part, -cos_part)
    slope_analysis = ((scale * number)[:, None] * (2.0 / points / norm) * slope_rows).T

    def rounded(t):
        return t.astype(np.float32).astype(ml_dtypes.bfloat16)

    return rounded(synthesis), rounded(analysis), rounded(slope_analysis)


def all_tables(ng, nr, npz):
    kxb = KXB * ng
    nkx, nkz = kxb * nr, KZB * npz
    syn_x, ana_x, slope_x = make_tables(nkx, nkx * 3 // 2, STREAM_SCALE)
    syn_z, ana_z, slope_z = make_tables(nkz, nkz * 3 // 2, SPAN_SCALE)
    r, c, m, g = np.meshgrid(
        np.arange(nr), np.arange(QUADS), np.arange(2), np.arange(ng), indexing="ij"
    )
    order = (g * (KXB * nr) + r * KXB + 2 * c + m).reshape(nr, kxb)
    plain = order.reshape(-1)
    crossed = order.reshape(nr // 2, 2, kxb)[:, ::-1].reshape(-1)
    rows = KZB * KXB
    move = np.zeros((rows, rows), np.float32)
    kz, kx = np.meshgrid(np.arange(KZB), np.arange(KXB), indexing="ij")
    move[(kz * KXB + kx).reshape(-1), (kx * KZB + kz).reshape(-1)] = 1.0
    return (
        move.astype(ml_dtypes.bfloat16),
        np.ascontiguousarray(syn_z.T),
        np.ascontiguousarray(syn_x[plain]),
        np.ascontiguousarray(syn_x[crossed]),
        np.ascontiguousarray(slope_x[:, plain]),
        np.ascontiguousarray(ana_x[:, crossed]),
        ana_z,
        slope_z,
    )


def dot(a, b, ca, cb):
    return lax.dot_general(a, b, (((ca,), (cb,)), ((), ())), preferred_element_type=F32)


def kernel_body(
    ng, nr, npz,
    slope_h, vort_h, vel_h, curv_h, vslope_h,
    move_h, synz_h, synx0_h, synx1_h, slopex_h, anax_h, anaz_h, slopez_h,
    basis_h, decay_h, mean_ref, visc_ref, dt_ref,
    out_ref,
    xin, move, synz, synx0, synx1, slopex, anax, anaz, slopez, basis_ref, decay_ref,
    stage, send_a, recv_a, wide, coef, mixed_rows, send_b, recv_b, lhs, grids, flux,
    send_c, recv_c, back, send_d, recv_d, old, spread,
    in_sem, tab_sem, sa_sem, ra_sem, sb_sem, rb_sem, sc_sem, rc_sem, sd_sem, rd_sem,
):
    owners = ng * npz
    kxl = KXB * ng
    zb = synz.shape[0] // nr
    nxp = synx0.shape[1]
    points = WALLS * owners
    px = lax.axis_index("px")
    pz = lax.axis_index("pz")
    g = px // nr
    r = px % nr
    me = pz * ng + g
    par = r % 2
    ny, nz = ng // 2, 2 * npz
    y = g // 2
    z = (g % 2) * npz + pz

    def each_owner(act):
        def at(dz, dy):
            z2 = (z + dz) % nz
            g2 = (y + dy) % ny * 2 + z2 // npz
            p2 = z2 % npz
            act(p2 * ng + g2, {"px": g2 * nr + r, "pz": p2})

        @pl.loop(0, nz - 1)
        def _(k):
            up, down = nz // 2 + (k + 1) // 2, nz // 2 - k // 2
            dz = k % 2 * up + (1 - k % 2) * down
            for dy in range(ny):
                at(dz, dy)

        for dy in range(1, ny):
            at(0, dy)

    def each_peer(act):
        @pl.loop(1, nr)
        def _(t):
            q = (r + t) % nr
            act(q, {"px": g * nr + q, "pz": pz})

    def remote(src, dst, send_sem, recv_sem, device):
        pltpu.make_async_remote_copy(
            src_ref=src, dst_ref=dst, send_sem=send_sem, recv_sem=recv_sem,
            device_id=device, device_id_type=pl.DeviceIdType.MESH,
        ).start()

    def await_all(ref, sem):
        pltpu.make_async_copy(ref, ref, sem).wait()

    barrier = pltpu.get_barrier_semaphore()

    def greet(_, device):
        pl.semaphore_signal(
            barrier, inc=1, device_id=device, device_id_type=pl.DeviceIdType.MESH
        )

    each_owner(greet)
    each_peer(greet)

    tabs = [
        pltpu.make_async_copy(h, v, tab_sem.at[i])
        for i, (h, v) in enumerate(
            (
                (move_h, move), (synz_h, synz), (synx0_h, synx0), (synx1_h, synx1),
                (slopex_h, slopex), (anax_h, anax), (anaz_h, anaz), (slopez_h, slopez),
                (basis_h, basis_ref), (decay_h, decay_ref),
            )
        )
    ]
    ins = [
        pltpu.make_async_copy(h, xin.at[i], in_sem.at[i])
        for i, h in enumerate((slope_h, vort_h, vel_h, curv_h, vslope_h))
    ]
    tabs[0].start()
    for copy in ins:
        copy.start()
    for copy in tabs[8:] + tabs[1:8]:
        copy.start()

    tabs[0].wait()
    per_owner = FIELDS * QUADS
    for i in range(FIELDS):
        ins[i].wait()
        block = xin[i].reshape(KZB * KXB, points)
        turned = dot(block, move[...], 0, 0)
        for j in range(WALLS):
            for c in range(QUADS):
                stage[pl.ds(j * owners * per_owner + i * QUADS + c, owners, stride=per_owner), :] = (
                    turned[j * owners : (j + 1) * owners, 128 * c : 128 * c + 128]
                )
        if i == VORT:
            old[...] = turned

    pieces = [(j, 0, FIELDS) for j in range(WALLS - 1)]
    pieces += [(WALLS - 1, 0, EARLY), (WALLS - 1, EARLY, FIELDS)]
    for n, (j, lo, hi) in enumerate(pieces):
        if lo == 0:
            rows = owners * per_owner
            send_a[j] = (
                stage[j * rows : (j + 1) * rows, :].astype(BF).reshape(owners, FIELDS, QUADS, 128)
            )
        if n == 0:
            pl.semaphore_wait(barrier, owners - 1 + nr - 1)
        pltpu.make_async_copy(
            send_a.at[j, me, pl.ds(lo, hi - lo)], recv_a.at[j, me, pl.ds(lo, hi - lo)], ra_sem.at[n]
        ).start()

        def send(to, device, n=n, j=j, part=pl.ds(lo, hi - lo)):
            remote(
                send_a.at[j, to, part], recv_a.at[j, me, part], sa_sem.at[n], ra_sem.at[n], device
            )

        each_owner(send)

    row = lax.broadcasted_iota(jnp.int32, (owners, 128), 0)
    lane = lax.broadcasted_iota(jnp.int32, (owners, 128), 1)
    lower = lane < KZB
    even = lane % 2 == 0
    kz_rate = SPAN_SCALE * ((KZB // 2) * (row // ng) + (lane % KZB) // 2).astype(F32)
    fz = jnp.where(even, kz_rate, -kz_rate)
    for c in range(QUADS):
        number = (KXB // 2) * nr * (row % ng) + (KXB // 2) * r + c
        kx_rate = STREAM_SCALE * number.astype(F32)
        fx = jnp.where(lower, kx_rate, -kx_rate)
        square = kx_rate * kx_rate + kz_rate * kz_rate
        safe = jnp.where(square == 0.0, 1.0, square)
        coef[c, 0] = fx
        coef[c, 1] = fx / safe
        coef[c, 2] = fz / safe
    coef[0, 3] = fz

    tabs[8].wait()
    tabs[9].wait()
    col = lax.broadcasted_iota(jnp.int32, (points, points * QUADS), 1)
    point = lax.broadcasted_iota(jnp.int32, (points, points * QUADS), 0)
    wide_basis = dot(
        basis_ref[...], jnp.where(col // QUADS == point, 1.0, 0.0).astype(BF), 0, 0
    )
    for c in range(QUADS):
        spread[c * points : (c + 1) * points, :] = jnp.where(
            col % QUADS == c, wide_basis, 0.0
        ).astype(BF)
    old[...] = dot(basis_ref[...], old[...].astype(BF), 0, 0)

    def swap_x(v):
        return pltpu.roll(v, KZB, 1)

    def swap_z(v):
        return jnp.where(even, pltpu.roll(v, 127, 1), pltpu.roll(v, 1, 1))

    first = (row == 0) & (lane == 0) & (r == 0)

    def unpack(j, lo, hi):
        rows = (hi - lo) * QUADS
        wide[0 : owners * rows, :] = (
            recv_a[j, :, lo:hi].reshape(owners * rows, 128).astype(F32)
        )
        return lambda i, c: wide[pl.ds((i - lo) * QUADS + c, owners, stride=rows), :]

    def place(f, c, field):
        at = pl.multiple_of((f + par - 2 * par * (f % 2)) * kxl + c * 2 * ng, 2 * ng)
        keep = lower[:ng]
        low, high = [], []
        for p in range(npz // 2):
            one = field[2 * p * ng : (2 * p + 1) * ng]
            two = field[(2 * p + 1) * ng : (2 * p + 2) * ng]
            low.append(jnp.where(keep, one, pltpu.roll(two, KZB, 1)))
            high.append(jnp.where(keep, pltpu.roll(one, KZB, 1), two))
        packed = jnp.concatenate(
            [jnp.concatenate(low, axis=1), jnp.concatenate(high, axis=1)], axis=0
        )
        mixed_rows[pl.ds(at, 2 * ng), :] = packed.astype(BF)

    def exchange_b(j, lo, hi):
        width = 2 * kxl
        made = dot(synz[...], mixed_rows[lo * width : hi * width, :], 1, 1).astype(BF)
        for b in range(lo, hi):
            send_b[j, b] = made[:, (b - lo) * width : (b - lo + 1) * width]
        part = pl.ds(lo, hi - lo)
        n = 2 * j + (lo > 0)

        def rows(q):
            return send_b.at[j, part, pl.ds(pl.multiple_of(q * zb, zb), zb)]

        pltpu.make_async_copy(rows(r), recv_b.at[j, r, part], rb_sem.at[n]).start()
        each_peer(
            lambda q, device: remote(
                rows(q), recv_b.at[j, r, part], sb_sem.at[n], rb_sem.at[n], device
            )
        )

    def mean(i, j):
        return jnp.where(first, mean_ref[i, owners * j + me], 0.0)

    def forward_early(j):
        load = unpack(j, 0, EARLY)
        for c in range(QUADS):
            s, o, v = load(SLOPE, c), load(VORT, c), load(VEL, c)
            a, b = coef[c, 1], coef[c, 2]
            stream_vel = swap_z(b * o) - swap_x(a * s)
            span_vel = -swap_z(b * s) - swap_x(a * o)
            if c == 0:
                stream_vel += mean(0, j)
                span_vel += mean(1, j)
            for f, field in enumerate((stream_vel, span_vel, v, o)):
                place(f, c, field)
        exchange_b(j, 0, 2)

    def forward_late(j):
        load = unpack(j, VEL, FIELDS)
        for c in range(QUADS):
            v, cv, q = load(VEL, c), load(CURV, c), load(VSLOPE, c)
            fx, a, b, fzz = coef[c, 0], coef[c, 1], coef[c, 2], coef[0, 3]
            stream_vort = swap_z(fzz * v - b * cv) - swap_x(a * q)
            span_vort = swap_x(a * cv - fx * v) - swap_z(b * q)
            if c == 0:
                stream_vort += mean(3, j)
                span_vort -= mean(2, j)
            place(4, c, stream_vort)
            place(5, c, span_vort)
        exchange_b(j, 2, 3)

    half = lax.broadcasted_iota(jnp.int32, (zb, 2 * kxl), 1) < kxl

    def gather_b(j, lo, hi):
        await_all(recv_b.at[j, :, pl.ds(lo, hi - lo)], rb_sem.at[2 * j + (lo > 0)])
        for b in range(lo, hi):
            for p in range(nr // 2):
                one, two = recv_b[j, 2 * p, b], recv_b[j, 2 * p + 1, b]
                to = slice(2 * p * kxl, 2 * (p + 1) * kxl)
                lhs[2 * b, :, to] = jnp.where(half, one, two)
                lhs[2 * b + 1, :, to] = jnp.where(half, two, one)

    def grid(f, cut):
        return dot(lhs[f], (synx0 if f % 2 == 0 else synx1)[:, cut], 1, 0)

    cuts = [slice(n, n + min(256, nxp)) for n in range(0, nxp, min(256, nxp))]

    def middle_early(j):
        gather_b(j, 0, 2)
        for cut in cuts:
            for f in range(4):
                grids[f, :, cut] = grid(f, cut)

    def middle_late(j):
        gather_b(j, 2, 3)
        for cut in cuts:
            v, o = grids[2, :, cut], grids[3, :, cut]
            flux[0, :, cut] = (grids[0, :, cut] * o - v * grid(4, cut)).astype(BF)
            flux[1, :, cut] = (grids[1, :, cut] * o - v * grid(5, cut)).astype(BF)
        for p in range(nr // 2):
            cut = slice(2 * p * kxl, 2 * (p + 1) * kxl)
            stream_part = dot(flux[0], slopex[:, cut], 1, 0)
            span_part = dot(flux[1], anax[:, cut], 1, 0)
            send_c[j, 2 * p] = jnp.where(half, stream_part, span_part).astype(BF)
            send_c[j, 2 * p + 1] = jnp.where(half, span_part, stream_part).astype(BF)
        pltpu.make_async_copy(send_c.at[j, r], recv_c.at[j, r], rc_sem.at[j]).start()
        each_peer(
            lambda q, device: remote(
                send_c.at[j, q], recv_c.at[j, r], sc_sem.at[j], rc_sem.at[j], device
            )
        )

    def backward(j):
        await_all(recv_c.at[j], rc_sem.at[j])
        parts = recv_c[j].reshape(nr * zb, 2 * kxl)
        one = dot(parts, anaz[...], 0, 0)
        two = dot(parts, slopez[...], 0, 0)
        nonlinear = -jnp.where(par == 0, one[:kxl] + two[kxl:], one[kxl:] + two[:kxl])
        keep = lower[:ng]
        for c in range(QUADS):
            for p in range(npz // 2):
                cut = slice(128 * p, 128 * p + 128)
                low = nonlinear[2 * c * ng : (2 * c + 1) * ng, cut]
                high = nonlinear[(2 * c + 1) * ng : (2 * c + 2) * ng, cut]
                back[pl.ds(2 * p * ng * QUADS + c, ng, stride=QUADS), :] = jnp.where(
                    keep, low, pltpu.roll(high, KZB, 1)
                )
                back[pl.ds((2 * p + 1) * ng * QUADS + c, ng, stride=QUADS), :] = jnp.where(
                    keep, pltpu.roll(low, KZB, 1), high
                )
        send_d[j] = back[...].astype(BF).reshape(owners, QUADS, 128)

    def exchange_d(j):
        pltpu.make_async_copy(send_d.at[j, me], recv_d.at[j, me], rd_sem.at[j]).start()
        each_owner(
            lambda to, device: remote(
                send_d.at[j, to], recv_d.at[j, me], sd_sem.at[j], rd_sem.at[j], device
            )
        )

    await_all(recv_a.at[0], ra_sem.at[0])
    tabs[1].wait()
    forward_early(0)
    forward_late(0)
    tabs[2].wait()
    tabs[3].wait()
    middle_early(0)
    tabs[4].wait()
    tabs[5].wait()
    middle_late(0)
    await_all(recv_a.at[1], ra_sem.at[1])
    forward_early(1)
    forward_late(1)
    tabs[6].wait()
    tabs[7].wait()
    backward(0)
    middle_early(1)
    middle_late(1)
    await_all(recv_a.at[2, :, pl.ds(0, EARLY)], ra_sem.at[2])
    forward_early(2)
    backward(1)
    await_all(recv_a.at[2, :, pl.ds(EARLY, FIELDS - EARLY)], ra_sem.at[3])
    forward_late(2)
    exchange_d(0)
    middle_early(2)
    middle_late(2)
    exchange_d(1)
    backward(2)
    exchange_d(2)

    decay = jnp.transpose(jnp.broadcast_to(decay_ref[...], (128, points)))
    lane1 = lax.broadcasted_iota(jnp.int32, (1, 128), 1)
    kz1 = SPAN_SCALE * ((KZB // 2) * pz + (lane1 % KZB) // 2).astype(F32)
    kz_square = kz1 * kz1
    for j in range(WALLS):
        await_all(recv_d.at[j], rd_sem.at[j])
    flux_coef = dot(spread[...], recv_d[...].reshape(points * QUADS, 128), 1, 0)
    solved = []
    for c in range(QUADS):
        kx1 = STREAM_SCALE * ((KXB // 2) * px + c).astype(F32)
        rates = decay + visc_ref[0] * (kz_square + kx1 * kx1)
        denom = 1.0 + IMPLICIT * rates
        old_coef = old[:, 128 * c : 128 * c + 128]
        new_coef = flux_coef[c * points : (c + 1) * points]
        mixed = (1.0 - EXPLICIT * rates) / denom * old_coef + FORCING * dt_ref[0] / denom * new_coef
        solved.append(dot(basis_ref[...], mixed.astype(BF), 1, 0).astype(BF))
    result = dot(move[...], jnp.concatenate(solved, axis=1), 1, 1)
    out_ref[...] = result.astype(BF).reshape(out_ref.shape)

    for n, (j, lo, hi) in enumerate(pieces):
        await_all(send_a.at[j, pl.ds(0, owners - 1), pl.ds(lo, hi - lo)], sa_sem.at[n])
    for j in range(WALLS):
        await_all(recv_b.at[j, pl.ds(0, nr - 1), pl.ds(0, 2)], sb_sem.at[2 * j])
        await_all(recv_b.at[j, pl.ds(0, nr - 1), pl.ds(2, 1)], sb_sem.at[2 * j + 1])
        await_all(send_c.at[j, pl.ds(0, nr - 1)], sc_sem.at[j])
        await_all(send_d.at[j, pl.ds(0, owners - 1)], sd_sem.at[j])


def per_device(
    ng, nr, npz, tables,
    wall_vel, wall_slope, wall_curvature, vorticity, vort_slope,
    mean_profile, eigen_basis, eigen_decay, viscous_step, time_step,
):
    owners = ng * npz
    kxl = KXB * ng
    nkx, nkz = kxl * nr, KZB * npz
    nxp, nzp = nkx * 3 // 2, nkz * 3 // 2
    zb = nzp // nr
    points = WALLS * owners
    lanes = KZB * KXB
    hbm = pl.BlockSpec(memory_space=pl.ANY)
    vmem = pl.BlockSpec(memory_space=pltpu.VMEM)
    smem = pl.BlockSpec(memory_space=pltpu.SMEM)
    dma = pltpu.SemaphoreType.DMA
    scratch = [
        pltpu.VMEM((FIELDS, KZB, KXB, points), BF),
        *[pltpu.VMEM(t.shape, BF) for t in tables],
        pltpu.VMEM((points, points), BF),
        pltpu.VMEM((1, points), F32),
        pltpu.VMEM((WALLS * owners * FIELDS * QUADS, 128), F32),
        pltpu.VMEM((WALLS, owners, FIELDS, QUADS, 128), BF),
        pltpu.VMEM((WALLS, owners, FIELDS, QUADS, 128), BF),
        pltpu.VMEM((owners * EARLY * QUADS, 128), F32),
        pltpu.VMEM((QUADS, 4, owners, 128), F32),
        pltpu.VMEM((6 * kxl, nkz), BF),
        pltpu.VMEM((WALLS, 3, nzp, 2 * kxl), BF),
        pltpu.VMEM((WALLS, nr, 3, zb, 2 * kxl), BF),
        pltpu.VMEM((6, zb, nkx), BF),
        pltpu.VMEM((4, zb, nxp), F32),
        pltpu.VMEM((2, zb, nxp), BF),
        pltpu.VMEM((WALLS, nr, zb, 2 * kxl), BF),
        pltpu.VMEM((WALLS, nr, zb, 2 * kxl), BF),
        pltpu.VMEM((owners * QUADS, 128), F32),
        pltpu.VMEM((WALLS, owners, QUADS, 128), BF),
        pltpu.VMEM((WALLS, owners, QUADS, 128), BF),
        pltpu.VMEM((points, lanes), F32),
        pltpu.VMEM((points * QUADS, points * QUADS), BF),
        dma((FIELDS,)),
        dma((len(tables) + 2,)),
        *[dma((WALLS + 1,)) for _ in range(2)],
        *[dma((2 * WALLS,)) for _ in range(2)],
        *[dma((WALLS,)) for _ in range(4)],
    ]
    out = pl.pallas_call(
        functools.partial(kernel_body, ng, nr, npz),
        out_shape=jax.ShapeDtypeStruct((lanes, points), BF),
        in_specs=[hbm] * (FIELDS + len(tables) + 2) + [smem] * 3,
        out_specs=vmem,
        scratch_shapes=scratch,
        compiler_params=pltpu.CompilerParams(
            collective_id=0, has_side_effects=True, vmem_limit_bytes=60 * 1024 * 1024
        ),
    )(
        wall_slope, vorticity, wall_vel, wall_curvature, vort_slope,
        *[jnp.asarray(t) for t in tables],
        eigen_basis, eigen_decay.reshape(1, points), mean_profile, viscous_step, time_step,
    )
    return out.reshape(vorticity.shape)


def build(mesh, nr):
    npz = mesh.shape["pz"]
    ng = mesh.shape["px"] // nr
    tables = all_tables(ng, nr, npz)
    spec = P("pz", "px", None)
    return jax.shard_map(
        functools.partial(per_device, ng, nr, npz, tables),
        mesh=mesh,
        in_specs=(spec,) * 5 + (P(),) * 5,
        out_specs=spec,
        check_vma=False,
    )


def solution(mesh):
    return build(mesh, NR)
```

time: 102 us -> 92.2 us (0.904)
  Pallas kernels: 96.9 us -> 89 us
  local copies, waits for them, and re-layouts: 3.11 us -> 1.67 us
    pallas_call x1, Pallas kernels: 96.9 us -> 89 us  [per_device(): pl.pallas_call(functools.partial(kernel_body, ng, nr, npz), out_shape=jax...]
    unnamed x3 -> x1, local copies, waits for them, and re-layouts: 2.34 us -> 1.67 us
where the time goes in v1:
time: 92.2 us; the launch traced here: 92 us
  Pallas kernels  89 us (97%)
  local copies, waits for them, and re-layouts  1.67 us (2%)
  between operations  1.3 us (1%)
    pallas_call x1, Pallas kernels, per_device(): pl.pallas_call(functools.partial(kernel_body, ng, nr, npz), out_shape=jax...  89 us

profile of v1, /device:TPU:1, one launch (start us, length us, event | category | flops | bytes accessed | tf_op | source)
XLA Modules:
  0.0 92.0 jit_solution(1010660120035514456)
XLA Ops:
  1.3 89.0 %shard_map.172 = bf16[512,192]{1,0:T(8,128)(2,1)} custom-call(bf16[64,8,192]{2,1,0:T(8,128)(2,1)} %slope_h.1, bf16[64,8,192]{2,1,0:T(8,128)(2,1)} %vort_h.1, bf16[64,8,192]{2,1,0:T(8,128)(2,1)} %vel_h.1, bf16[64,8,192]{2,1,0:T(8,128)(2,1)} %curv_h.1, bf16[64,8,192]{2,1,0:T(8,128)(2,1)} %vslope_h.1, bf16[512,512]{1,0:T(8,128)(2,1)} %constant.16.clone.move_h, ...), custom_call_target="tpu_custom_call" | custom-call | tf_op jit(solution)/shard_map/pallas_call | solution.py:487
  90.3 1.7 %copy.22 = bf16[64,8,192]{2,1,0:T(8,128)(2,1)} copy(bf16[64,8,192]{2,1,0:T(8,128)(2,1)} %bitcast.2) | data formatting | bytes 393216

commit v2 on v1

--- a/solution.py
+++ b/solution.py
@@ -85,11 +85,12 @@
     ng, nr, npz,
     slope_h, vort_h, vel_h, curv_h, vslope_h,
     move_h, synz_h, synx0_h, synx1_h, slopex_h, anax_h, anaz_h, slopez_h,
-    basis_h, decay_h, mean_ref, visc_ref, dt_ref,
+    basis_h, decay_h, mean_h, visc_h, dt_h,
     out_ref,
     xin, move, synz, synx0, synx1, slopex, anax, anaz, slopez, basis_ref, decay_ref,
+    mean_ref, visc_ref, dt_ref,
     stage, send_a, recv_a, wide, coef, mixed_rows, send_b, recv_b, lhs, grids, flux,
-    send_c, recv_c, back, send_d, recv_d, old, spread,
+    send_c, recv_c, back, send_d, recv_d, old, gain, flux_coef, spread,
     in_sem, tab_sem, sa_sem, ra_sem, sb_sem, rb_sem, sc_sem, rc_sem, sd_sem, rd_sem,
 ):
     owners = ng * npz
@@ -108,6 +109,8 @@
     z = (g % 2) * npz + pz
 
     def each_owner(act):
+        far_first = sorted(range(ny), key=lambda dy: -min(dy, ny - dy))
+
         def at(dz, dy):
             z2 = (z + dz) % nz
             g2 = (y + dy) % ny * 2 + z2 // npz
@@ -118,15 +121,14 @@
         def _(k):
             up, down = nz // 2 + (k + 1) // 2, nz // 2 - k // 2
             dz = k % 2 * up + (1 - k % 2) * down
-            for dy in range(ny):
+            for dy in far_first:
                 at(dz, dy)
 
-        for dy in range(1, ny):
+        for dy in far_first[:-1]:
             at(0, dy)
 
     def each_peer(act):
-        @pl.loop(1, nr)
-        def _(t):
+        for t in sorted(range(1, nr), key=lambda t: -min(t, nr - t)):
             q = (r + t) % nr
             act(q, {"px": g * nr + q, "pz": pz})
 
@@ -135,6 +137,9 @@
             src_ref=src, dst_ref=dst, send_sem=send_sem, recv_sem=recv_sem,
             device_id=device, device_id_type=pl.DeviceIdType.MESH,
         ).start()
+
+    def local(src, dst, sem):
+        pltpu.make_async_copy(src, dst, sem).start()
 
     def await_all(ref, sem):
         pltpu.make_async_copy(ref, ref, sem).wait()
@@ -156,6 +161,7 @@
                 (move_h, move), (synz_h, synz), (synx0_h, synx0), (synx1_h, synx1),
                 (slopex_h, slopex), (anax_h, anax), (anaz_h, anaz), (slopez_h, slopez),
                 (basis_h, basis_ref), (decay_h, decay_ref),
+                (mean_h, mean_ref), (visc_h, visc_ref), (dt_h, dt_ref),
             )
         )
     ]
@@ -193,11 +199,10 @@
             )
         if n == 0:
             pl.semaphore_wait(barrier, owners - 1 + nr - 1)
-        pltpu.make_async_copy(
-            send_a.at[j, me, pl.ds(lo, hi - lo)], recv_a.at[j, me, pl.ds(lo, hi - lo)], ra_sem.at[n]
-        ).start()
-
-        def send(to, device, n=n, j=j, part=pl.ds(lo, hi - lo)):
+        part = pl.ds(lo, hi - lo)
+        local(send_a.at[j, me, part], recv_a.at[j, me, part], ra_sem.at[n])
+
+        def send(to, device, n=n, j=j, part=part):
             remote(
                 send_a.at[j, to, part], recv_a.at[j, me, part], sa_sem.at[n], ra_sem.at[n], device
             )
@@ -221,8 +226,8 @@
         coef[c, 2] = fz / safe
     coef[0, 3] = fz
 
-    tabs[8].wait()
-    tabs[9].wait()
+    for copy in tabs[8:]:
+        copy.wait()
     col = lax.broadcasted_iota(jnp.int32, (points, points * QUADS), 1)
     point = lax.broadcasted_iota(jnp.int32, (points, points * QUADS), 0)
     wide_basis = dot(
@@ -274,7 +279,7 @@
         def rows(q):
             return send_b.at[j, part, pl.ds(pl.multiple_of(q * zb, zb), zb)]
 
-        pltpu.make_async_copy(rows(r), recv_b.at[j, r, part], rb_sem.at[n]).start()
+        local(rows(r), recv_b.at[j, r, part], rb_sem.at[n])
         each_peer(
             lambda q, device: remote(
                 rows(q), recv_b.at[j, r, part], sb_sem.at[n], rb_sem.at[n], device
@@ -340,17 +345,25 @@
             v, o = grids[2, :, cut], grids[3, :, cut]
             flux[0, :, cut] = (grids[0, :, cut] * o - v * grid(4, cut)).astype(BF)
             flux[1, :, cut] = (grids[1, :, cut] * o - v * grid(5, cut)).astype(BF)
-        for p in range(nr // 2):
-            cut = slice(2 * p * kxl, 2 * (p + 1) * kxl)
+        for t in sorted(range(nr // 2), key=lambda t: -min(t, nr // 2 - t)):
+            pair = (r // 2 + t) % (nr // 2)
+            cut = pl.ds(pl.multiple_of(2 * pair * kxl, 2 * kxl), 2 * kxl)
             stream_part = dot(flux[0], slopex[:, cut], 1, 0)
             span_part = dot(flux[1], anax[:, cut], 1, 0)
-            send_c[j, 2 * p] = jnp.where(half, stream_part, span_part).astype(BF)
-            send_c[j, 2 * p + 1] = jnp.where(half, span_part, stream_part).astype(BF)
-        pltpu.make_async_copy(send_c.at[j, r], recv_c.at[j, r], rc_sem.at[j]).start()
-        each_peer(
-            lambda q, device: remote(
-                send_c.at[j, q], recv_c.at[j, r], sc_sem.at[j], rc_sem.at[j], device
-            )
+            send_c[j, 2 * pair] = jnp.where(half, stream_part, span_part).astype(BF)
+            send_c[j, 2 * pair + 1] = jnp.where(half, span_part, stream_part).astype(BF)
+            if t == 0:
+                continue
+            for q in (2 * pair + par, 2 * pair + 1 - par):
+                remote(
+                    send_c.at[j, q], recv_c.at[j, r], sc_sem.at[j], rc_sem.at[j],
+                    {"px": g * nr + q, "pz": pz},
+                )
+        local(send_c.at[j, r], recv_c.at[j, r], rc_sem.at[j])
+        q = r + 1 - 2 * par
+        remote(
+            send_c.at[j, q], recv_c.at[j, r], sc_sem.at[j], rc_sem.at[j],
+            {"px": g * nr + q, "pz": pz},
         )
 
     def backward(j):
@@ -374,7 +387,7 @@
         send_d[j] = back[...].astype(BF).reshape(owners, QUADS, 128)
 
     def exchange_d(j):
-        pltpu.make_async_copy(send_d.at[j, me], recv_d.at[j, me], rd_sem.at[j]).start()
+        local(send_d.at[j, me], recv_d.at[j, me], rd_sem.at[j])
         each_owner(
             lambda to, device: remote(
                 send_d.at[j, to], recv_d.at[j, me], sd_sem.at[j], rd_sem.at[j], device
@@ -415,17 +428,27 @@
     lane1 = lax.broadcasted_iota(jnp.int32, (1, 128), 1)
     kz1 = SPAN_SCALE * ((KZB // 2) * pz + (lane1 % KZB) // 2).astype(F32)
     kz_square = kz1 * kz1
-    for j in range(WALLS):
-        await_all(recv_d.at[j], rd_sem.at[j])
-    flux_coef = dot(spread[...], recv_d[...].reshape(points * QUADS, 128), 1, 0)
-    solved = []
     for c in range(QUADS):
+        lanes = slice(128 * c, 128 * c + 128)
         kx1 = STREAM_SCALE * ((KXB // 2) * px + c).astype(F32)
         rates = decay + visc_ref[0] * (kz_square + kx1 * kx1)
         denom = 1.0 + IMPLICIT * rates
-        old_coef = old[:, 128 * c : 128 * c + 128]
-        new_coef = flux_coef[c * points : (c + 1) * points]
-        mixed = (1.0 - EXPLICIT * rates) / denom * old_coef + FORCING * dt_ref[0] / denom * new_coef
+        old[:, lanes] = (1.0 - EXPLICIT * rates) / denom * old[:, lanes]
+        gain[:, lanes] = FORCING * dt_ref[0] / denom
+    ready = owners * QUADS * (WALLS - 1)
+    for j in range(WALLS - 1):
+        await_all(recv_d.at[j], rd_sem.at[j])
+    before = recv_d[: WALLS - 1].reshape(ready, 128)
+    for c in range(QUADS):
+        lanes, rows = slice(128 * c, 128 * c + 128), slice(c * points, (c + 1) * points)
+        flux_coef[:, lanes] = dot(spread[rows, :ready], before, 1, 0)
+    await_all(recv_d.at[WALLS - 1], rd_sem.at[WALLS - 1])
+    last = recv_d[WALLS - 1].reshape(owners * QUADS, 128)
+    solved = []
+    for c in range(QUADS):
+        lanes, rows = slice(128 * c, 128 * c + 128), slice(c * points, (c + 1) * points)
+        new_coef = flux_coef[:, lanes] + dot(spread[rows, ready:], last, 1, 0)
+        mixed = old[:, lanes] + gain[:, lanes] * new_coef
         solved.append(dot(basis_ref[...], mixed.astype(BF), 1, 0).astype(BF))
     result = dot(move[...], jnp.concatenate(solved, axis=1), 1, 1)
     out_ref[...] = result.astype(BF).reshape(out_ref.shape)
@@ -451,15 +474,17 @@
     zb = nzp // nr
     points = WALLS * owners
     lanes = KZB * KXB
-    hbm = pl.BlockSpec(memory_space=pl.ANY)
+    hbm = pl.BlockSpec(memory_space=pltpu.HBM)
     vmem = pl.BlockSpec(memory_space=pltpu.VMEM)
-    smem = pl.BlockSpec(memory_space=pltpu.SMEM)
     dma = pltpu.SemaphoreType.DMA
     scratch = [
         pltpu.VMEM((FIELDS, KZB, KXB, points), BF),
         *[pltpu.VMEM(t.shape, BF) for t in tables],
         pltpu.VMEM((points, points), BF),
         pltpu.VMEM((1, points), F32),
+        pltpu.SMEM(mean_profile.shape, F32),
+        pltpu.SMEM((1,), F32),
+        pltpu.SMEM((1,), F32),
         pltpu.VMEM((WALLS * owners * FIELDS * QUADS, 128), F32),
         pltpu.VMEM((WALLS, owners, FIELDS, QUADS, 128), BF),
         pltpu.VMEM((WALLS, owners, FIELDS, QUADS, 128), BF),
@@ -477,17 +502,19 @@
         pltpu.VMEM((WALLS, owners, QUADS, 128), BF),
         pltpu.VMEM((WALLS, owners, QUADS, 128), BF),
         pltpu.VMEM((points, lanes), F32),
+        pltpu.VMEM((points, lanes), F32),
+        pltpu.VMEM((points, lanes), F32),
         pltpu.VMEM((points * QUADS, points * QUADS), BF),
         dma((FIELDS,)),
-        dma((len(tables) + 2,)),
+        dma((len(tables) + 5,)),
         *[dma((WALLS + 1,)) for _ in range(2)],
         *[dma((2 * WALLS,)) for _ in range(2)],
         *[dma((WALLS,)) for _ in range(4)],
     ]
     out = pl.pallas_call(
         functools.partial(kernel_body, ng, nr, npz),
-        out_shape=jax.ShapeDtypeStruct((lanes, points), BF),
-        in_specs=[hbm] * (FIELDS + len(tables) + 2) + [smem] * 3,
+        out_shape=pltpu.VMEM((lanes, points), BF),
+        in_specs=[hbm] * (FIELDS + len(tables) + 5),
         out_specs=vmem,
         scratch_shapes=scratch,
         compiler_params=pltpu.CompilerParams(

time: 92.2 us -> 87.6 us (0.950)
  Pallas kernels: 89 us -> 85.5 us
  local copies, waits for them, and re-layouts: 1.67 us -> 0.71 us
    pallas_call x1, Pallas kernels: 89 us -> 85.5 us  [per_device(): pl.pallas_call(functools.partial(kernel_body, ng, nr, npz), out_shape=plt...]
    unnamed x1, local copies, waits for them, and re-layouts: 1.67 us -> 0.71 us
where the time goes in v2:
time: 87.6 us; the launch traced here: 87.5 us
  Pallas kernels  85.5 us (98%)
  between operations  1.3 us (1%)
    pallas_call x1, Pallas kernels, per_device(): pl.pallas_call(functools.partial(kernel_body, ng, nr, npz), out_shape=plt...  85.5 us

profile of v2, /device:TPU:1, one launch (start us, length us, event | category | flops | bytes accessed | tf_op | source)
XLA Modules:
  0.0 87.5 jit_solution(4084460493246752263)
XLA Ops:
  1.3 85.5 %shard_map.172 = bf16[512,192]{1,0:T(8,128)(2,1)S(1)} custom-call(bf16[64,8,192]{2,1,0:T(8,128)(2,1)} %slope_h.1, bf16[64,8,192]{2,1,0:T(8,128)(2,1)} %vort_h.1, bf16[64,8,192]{2,1,0:T(8,128)(2,1)} %vel_h.1, bf16[64,8,192]{2,1,0:T(8,128)(2,1)} %curv_h.1, bf16[64,8,192]{2,1,0:T(8,128)(2,1)} %vslope_h.1, bf16[512,512]{1,0:T(8,128)(2,1)} %constant.16.clone.move_h, ...), custom_call_target="tpu_custom_call" | custom-call | tf_op jit(solution)/shard_map/pallas_call | solution.py:514
  86.8 0.7 copy.20

commit v3 on v2

--- a/solution.py
+++ b/solution.py
@@ -172,8 +172,6 @@
     tabs[0].start()
     for copy in ins:
         copy.start()
-    for copy in tabs[8:] + tabs[1:8]:
-        copy.start()
 
     tabs[0].wait()
     per_owner = FIELDS * QUADS
@@ -188,6 +186,9 @@
                 )
         if i == VORT:
             old[...] = turned
+
+    for copy in tabs[8:] + tabs[1:8]:
+        copy.start()
 
     pieces = [(j, 0, FIELDS) for j in range(WALLS - 1)]
     pieces += [(WALLS - 1, 0, EARLY), (WALLS - 1, EARLY, FIELDS)]
@@ -339,7 +340,13 @@
             for f in range(4):
                 grids[f, :, cut] = grid(f, cut)
 
-    def middle_late(j):
+    def exchange_c(j, q):
+        remote(
+            send_c.at[j, q], recv_c.at[j, r], sc_sem.at[j], rc_sem.at[j],
+            {"px": g * nr + q, "pz": pz},
+        )
+
+    def middle_late(j, held=False):
         gather_b(j, 2, 3)
         for cut in cuts:
             v, o = grids[2, :, cut], grids[3, :, cut]
@@ -352,19 +359,12 @@
             span_part = dot(flux[1], anax[:, cut], 1, 0)
             send_c[j, 2 * pair] = jnp.where(half, stream_part, span_part).astype(BF)
             send_c[j, 2 * pair + 1] = jnp.where(half, span_part, stream_part).astype(BF)
-            if t == 0:
-                continue
-            for q in (2 * pair + par, 2 * pair + 1 - par):
-                remote(
-                    send_c.at[j, q], recv_c.at[j, r], sc_sem.at[j], rc_sem.at[j],
-                    {"px": g * nr + q, "pz": pz},
-                )
+            if t > 0 and not held:
+                exchange_c(j, 2 * pair + par)
+                exchange_c(j, 2 * pair + 1 - par)
         local(send_c.at[j, r], recv_c.at[j, r], rc_sem.at[j])
-        q = r + 1 - 2 * par
-        remote(
-            send_c.at[j, q], recv_c.at[j, r], sc_sem.at[j], rc_sem.at[j],
-            {"px": g * nr + q, "pz": pz},
-        )
+        if not held:
+            exchange_c(j, r + 1 - 2 * par)
 
     def backward(j):
         await_all(recv_c.at[j], rc_sem.at[j])
@@ -410,16 +410,17 @@
     tabs[6].wait()
     tabs[7].wait()
     backward(0)
-    middle_early(1)
-    middle_late(1)
     await_all(recv_a.at[2, :, pl.ds(0, EARLY)], ra_sem.at[2])
     forward_early(2)
-    backward(1)
+    middle_early(1)
+    middle_late(1, held=True)
     await_all(recv_a.at[2, :, pl.ds(EARLY, FIELDS - EARLY)], ra_sem.at[3])
     forward_late(2)
+    each_peer(lambda q, _: exchange_c(1, q))
     exchange_d(0)
     middle_early(2)
     middle_late(2)
+    backward(1)
     exchange_d(1)
     backward(2)
     exchange_d(2)

time: 87.6 us -> 86.9 us (level)
  no operation moved by 1% of the time
where the time goes in v3:
time: 86.9 us; the launch traced here: 86.7 us
  Pallas kernels  84.7 us (97%)
  between operations  1.3 us (1%)
    pallas_call x1, Pallas kernels, per_device(): pl.pallas_call(functools.partial(kernel_body, ng, nr, npz), out_shape=plt...  84.7 us

profile of v3, /device:TPU:1, one launch (start us, length us, event | category | flops | bytes accessed | tf_op | source)
XLA Modules:
  0.0 86.7 jit_solution(9518994367312356203)
XLA Ops:
  1.3 84.7 %shard_map.172 = bf16[512,192]{1,0:T(8,128)(2,1)S(1)} custom-call(bf16[64,8,192]{2,1,0:T(8,128)(2,1)} %slope_h.1, bf16[64,8,192]{2,1,0:T(8,128)(2,1)} %vort_h.1, bf16[64,8,192]{2,1,0:T(8,128)(2,1)} %vel_h.1, bf16[64,8,192]{2,1,0:T(8,128)(2,1)} %curv_h.1, bf16[64,8,192]{2,1,0:T(8,128)(2,1)} %vslope_h.1, bf16[512,512]{1,0:T(8,128)(2,1)} %constant.16.clone.move_h, ...), custom_call_target="tpu_custom_call" | custom-call | tf_op jit(solution)/shard_map/pallas_call | solution.py:515
  86.0 0.7 copy.20

commit v4 on v3

--- a/solution.py
+++ b/solution.py
@@ -107,29 +107,31 @@
     ny, nz = ng // 2, 2 * npz
     y = g // 2
     z = (g % 2) * npz + pz
+    rows_g = [lax.rem(y + dy, ny) * 2 for dy in range(ny)]
 
     def each_owner(act):
         far_first = sorted(range(ny), key=lambda dy: -min(dy, ny - dy))
 
-        def at(dz, dy):
-            z2 = (z + dz) % nz
-            g2 = (y + dy) % ny * 2 + z2 // npz
-            p2 = z2 % npz
-            act(p2 * ng + g2, {"px": g2 * nr + r, "pz": p2})
+        def at(dz, dys):
+            z2 = lax.rem(z + dz, nz)
+            high = lax.div(z2, npz)
+            p2 = z2 - high * npz
+            to = p2 * ng + high
+            place = high * nr + r
+            for dy in dys:
+                act(to + rows_g[dy], {"px": place + rows_g[dy] * nr, "pz": p2})
 
         @pl.loop(0, nz - 1)
         def _(k):
-            up, down = nz // 2 + (k + 1) // 2, nz // 2 - k // 2
-            dz = k % 2 * up + (1 - k % 2) * down
-            for dy in far_first:
-                at(dz, dy)
-
-        for dy in far_first[:-1]:
-            at(0, dy)
+            half = lax.div(k + 1, 2)
+            up = half + half - k
+            at(nz // 2 + up * half - (1 - up) * half, far_first)
+
+        at(0, far_first[:-1])
 
     def each_peer(act):
         for t in sorted(range(1, nr), key=lambda t: -min(t, nr - t)):
-            q = (r + t) % nr
+            q = lax.rem(r + t, nr)
             act(q, {"px": g * nr + q, "pz": pz})
 
     def remote(src, dst, send_sem, recv_sem, device):

time: 86.9 us -> 86.8 us (level)
  no operation moved by 1% of the time
where the time goes in v4:
time: 86.8 us; the launch traced here: 86.6 us
  Pallas kernels  84.6 us (97%)
  between operations  1.3 us (1%)
    pallas_call x1, Pallas kernels, per_device(): pl.pallas_call(functools.partial(kernel_body, ng, nr, npz), out_shape=plt...  84.6 us

profile of v4, /device:TPU:1, one launch (start us, length us, event | category | flops | bytes accessed | tf_op | source)
XLA Modules:
  0.0 86.6 jit_solution(17778928108493030026)
XLA Ops:
  1.3 84.6 %shard_map.172 = bf16[512,192]{1,0:T(8,128)(2,1)S(1)} custom-call(bf16[64,8,192]{2,1,0:T(8,128)(2,1)} %slope_h.1, bf16[64,8,192]{2,1,0:T(8,128)(2,1)} %vort_h.1, bf16[64,8,192]{2,1,0:T(8,128)(2,1)} %vel_h.1, bf16[64,8,192]{2,1,0:T(8,128)(2,1)} %curv_h.1, bf16[64,8,192]{2,1,0:T(8,128)(2,1)} %vslope_h.1, bf16[512,512]{1,0:T(8,128)(2,1)} %constant.16.clone.move_h, ...), custom_call_target="tpu_custom_call" | custom-call | tf_op jit(solution)/shard_map/pallas_call | solution.py:517
  85.9 0.7 copy.20
